TPU v7x, 32 devices: a whole 2x2x4 slice. The times are simulated.
32 devices in a mesh: lon: 8 (over y, x, core), lat: 4 (over z).
Axes of the slice: x: 2, y: 2, z: 4, core: 2. Of those that a mesh axis runs over, the one named last changes fastest.
Arguments:
- thermal_anomaly: float32 [8, 128, 1024], P(None, 'lat', 'lon'), may hold values from -6 to 6
- saltiness_anomaly: float32 [8, 128, 1024], P(None, 'lat', 'lon'), may hold values from -6 to 6
- zonal_velocity: float32 [8, 128, 1024], P(None, 'lat', 'lon'), may hold values from -3 to 3
- meridional_velocity: float32 [8, 128, 1024], P(None, 'lat', 'lon'), may hold values from -3 to 3
- sea_point_indicator: int32 [8, 128, 1024], P(None, 'lat', 'lon'), may hold values 0 or 1
Outputs:
- temperature_out: float32 [8, 128, 1024], P(None, 'lat', 'lon')
- salinity_out: float32 [8, 128, 1024], P(None, 'lat', 'lon')
- east_out: float32 [8, 128, 1024], P(None, 'lat', 'lon')
- north_out: float32 [8, 128, 1024], P(None, 'lat', 'lon')
All inputs are finite; a program needn't handle non-finite values. No bound on the sum of `sea_point_indicator` on one device may be relied on, other than what follows from the above.
Results may differ from a plain program's by a relative error of at most 0.00002.
Values sent between devices are 32-bit elements; how exact they have to be, the bound alone decides.
A program may use at most 64 MiB of HBM per device.

v0:
```python
import jax
import jax.numpy as jnp
from jax import lax
from jax.sharding import PartitionSpec as P

STEPS = 2


time_step = 0.8
diffusivity = 0.15
pressure_gain = 0.12
layer_depth = 0.5


def with_halo(value, sides, width, wrap):
    for axis, dim in sides:
        devices, length = (lax.axis_size(axis), value.shape[dim])
        up = [(i, (i + 1) % devices) for i in range(devices if wrap else devices - 1)]
        down = [(j, i) for i, j in up]
        last = lax.slice_in_dim(value, length - width, length, axis=dim)
        first = lax.slice_in_dim(value, 0, width, axis=dim)
        before = lax.ppermute(last, axis, up)
        after = lax.ppermute(first, axis, down)
        value = jnp.concatenate([before, value, after], axis=dim)
    return value


def hydrostatic_force(temp_field, salt_field):
    density = 0.8 * salt_field - 0.2 * temp_field
    return jnp.cumsum(density, axis=0) * layer_depth


def velocity(east_field, north_field, hydrostatic_load, sea_share_factor):
    grad_east = hydrostatic_load[:, 1:-1, 2:] - hydrostatic_load[:, 1:-1, :-2]
    grad_north = hydrostatic_load[:, 2:, 1:-1] - hydrostatic_load[:, :-2, 1:-1]
    zonal_velocity_next = (east_field - pressure_gain * grad_east) * sea_share_factor
    meridional_velocity_next = (north_field - pressure_gain * grad_north) * sea_share_factor
    return (zonal_velocity_next, meridional_velocity_next)


def advected_scalar(tracer_field, east_field, north_field, sea_share_factor):
    rows_q = tracer_field[:, 1:-1, :]
    rows_u = east_field[:, 1:-1, :]
    rows_m = sea_share_factor[:, 1:-1, :]
    flux_east = 0.25 * (rows_u[..., :-1] + rows_u[..., 1:]) * (rows_q[..., :-1] + rows_q[..., 1:])
    flux_east = (
        (flux_east - diffusivity * (rows_q[..., 1:] - rows_q[..., :-1]))
        * rows_m[..., :-1]
        * rows_m[..., 1:]
    )
    cols_q = tracer_field[:, :, 1:-1]
    cols_v = north_field[:, :, 1:-1]
    cols_m = sea_share_factor[:, :, 1:-1]
    flux_north = 0.25 * (cols_v[:, :-1] + cols_v[:, 1:]) * (cols_q[:, :-1] + cols_q[:, 1:])
    flux_north = (
        (flux_north - diffusivity * (cols_q[:, 1:] - cols_q[:, :-1]))
        * cols_m[:, :-1]
        * cols_m[:, 1:]
    )
    divergence = flux_east[..., 1:] - flux_east[..., :-1] + flux_north[:, 1:] - flux_north[:, :-1]
    return tracer_field[:, 1:-1, 1:-1] - time_step * sea_share_factor[:, 1:-1, 1:-1] * divergence


def mirror_partner(slab):
    slab_shape = slab.shape
    device_count = lax.axis_size("lon")
    flat = slab.reshape(1, -1)
    received = lax.all_to_all(flat, "lon", split_axis=1, concat_axis=1, tiled=True)
    items = received.shape[0]
    blocks = received.reshape(items, device_count, -1)
    turned = jnp.flip(blocks, axis=1).reshape(items, -1)
    arrived = lax.all_to_all(turned, "lon", split_axis=1, concat_axis=1, tiled=True)
    return arrived.reshape(slab_shape)


def enlarge_by_margin(fields, signs, margin):
    row_count = fields.shape[2]
    sign_column = jnp.array(signs, dtype=jnp.float32)[:, None, None, None]
    with_rows = with_halo(fields, (("lat", 2),), margin, False)
    fold_slab = jnp.flip(fields[:, :, row_count - margin :, :], axis=(2, 3)) * sign_column
    fold_slab = mirror_partner(fold_slab)
    at_north = lax.axis_index("lat") == lax.axis_size("lat") - 1
    folded = jnp.concatenate([with_rows[:, :, : row_count + margin], fold_slab], axis=2)
    with_rows = jnp.where(at_north, folded, with_rows)
    return with_halo(with_rows, (("lon", 3),), margin, True)


def shards(
    thermal_anomaly, saltiness_anomaly, zonal_velocity, meridional_velocity, sea_point_indicator
):
    wet_own = sea_point_indicator.astype(jnp.float32)
    sea_share_factor = enlarge_by_margin(wet_own[None], (1.0,), 1)[0]
    for repeat in range(STEPS):
        scalars_enlarged = enlarge_by_margin(
            jnp.stack([thermal_anomaly, saltiness_anomaly]), (1.0, 1.0), 1
        )
        hydrostatic_load = hydrostatic_force(scalars_enlarged[0], scalars_enlarged[1])
        zonal_velocity, meridional_velocity = velocity(
            zonal_velocity, meridional_velocity, hydrostatic_load, wet_own
        )
        widened_flows = enlarge_by_margin(
            jnp.stack([zonal_velocity, meridional_velocity]), (-1.0, -1.0), 1
        )
        thermal_anomaly = advected_scalar(
            scalars_enlarged[0], widened_flows[0], widened_flows[1], sea_share_factor
        )
        saltiness_anomaly = advected_scalar(
            scalars_enlarged[1], widened_flows[0], widened_flows[1], sea_share_factor
        )
    return (thermal_anomaly, saltiness_anomaly, zonal_velocity, meridional_velocity)


def solution(mesh):
    return jax.shard_map(
        shards,
        mesh=mesh,
        in_specs=(
            P(None, "lat", "lon"),
            P(None, "lat", "lon"),
            P(None, "lat", "lon"),
            P(None, "lat", "lon"),
            P(None, "lat", "lon"),
        ),
        out_specs=(
            P(None, "lat", "lon"),
            P(None, "lat", "lon"),
            P(None, "lat", "lon"),
            P(None, "lat", "lon"),
        ),
        check_vma=False,
    )
```

profile of v0, /device:TPU:0, one launch (start us, length us, event | category | flops | bytes accessed | tf_op | source)
XLA Modules:
  0.0 142.1 jit_solution(2028672826668283988)
XLA Ops:
  2.5 5.2 %all-to-all-start = ((f32[1,8,256]{2,0,1:T(1,128)}), f32[1,8,256]{2,0,1:T(1,128)S(1)}, u32[]{:S(2)}, u32[]{:S(2)}) async-start(f32[1,8,256]{2,0,1:T(1,128)} %bitcast.2), calls=%async_computation | async-start | bytes 16384 | tf_op jit(solution)/shard_map/all_to_all | solution.py:68
  8.4 3.9 %all-to-all-done = f32[1,8,256]{2,0,1:T(1,128)S(1)} async-done(((f32[1,8,256]{2,0,1:T(1,128)}), f32[1,8,256]{2,0,1:T(1,128)S(1)}, u32[]{:S(2)}, u32[]{:S(2)}) %all-to-all-start) | async-done | bytes 8224 | tf_op jit(solution)/shard_map/all_to_all | solution.py:68
  12.3 3.3 %all-to-all-start.2 = ((f32[1,8,128]{2,0,1:T(1,128)}), f32[1,8,128]{2,0,1:T(1,128)S(1)}, u32[]{:S(2)}, u32[]{:S(2)}) async-start(f32[1,8,128]{2,0,1:T(1,128)} %bitcast.7), calls=%async_computation.2 | async-start | bytes 8192 | tf_op jit(solution)/shard_map/all_to_all | solution.py:68
  15.6 3.5 %collective-permute-start = (f32[2,8,1,128]{3,1,2,0:T(8,128)S(1)}, f32[2,8,1,128]{3,1,2,0:T(8,128)S(1)}, u32[]{:S(2)}, u32[]{:S(2)}) collective-permute-start(f32[2,8,1,128]{3,1,2,0:T(8,128)S(1)} %get-tuple-element.47), channel_id=1, source_target_pairs={{0,1},{1,2},{2,3},{4,5},{5,6},{6,7},{8,9},{9,10},{10,11},{12,13},{... | collective-permute-start | bytes 24584 | tf_op jit(solution)/shard_map/ppermute | solution.py:22
  21.1 4.1 %all-to-all-start.1 = ((f32[1,8,256]{2,0,1:T(1,128)}), f32[1,8,256]{2,0,1:T(1,128)S(1)}, u32[]{:S(2)}, u32[]{:S(2)}) async-start(f32[1,8,256]{2,0,1:T(1,128)} %all_to_all.62), calls=%async_computation.1 | async-start | bytes 16384 | tf_op jit(solution)/shard_map/all_to_all | solution.py:72
  25.2 4.5 %collective-permute-start.4 = (f32[1,8,1,128]{3,1,2,0:T(8,128)S(1)}, f32[1,8,1,128]{3,1,2,0:T(8,128)S(1)}, u32[]{:S(2)}, u32[]{:S(2)}) collective-permute-start(f32[1,8,1,128]{3,1,2,0:T(8,128)S(1)} %get-tuple-element.51), channel_id=1, source_target_pairs={{0,1},{1,2},{2,3},{4,5},{5,6},{6,7},{8,9},{9,10},{10,11},{12,13},{... | collective-permute-start | bytes 12296 | tf_op jit(solution)/shard_map/ppermute | solution.py:22
  31.6 4.2 %all-to-all-start.3 = ((f32[1,8,128]{2,0,1:T(1,128)}), f32[1,8,128]{2,0,1:T(1,128)S(1)}, u32[]{:S(2)}, u32[]{:S(2)}) async-start(f32[1,8,128]{2,0,1:T(1,128)} %all_to_all.66), calls=%async_computation.3 | async-start | bytes 8192 | tf_op jit(solution)/shard_map/all_to_all | solution.py:72
  40.4 3.2 %collective-permute-done.2 = f32[2,8,34,1]{3,1,2,0:T(8,128)S(1)} collective-permute-done((f32[2,8,34,1]{3,1,2,0:T(8,128)S(1)}, f32[2,8,34,1]{3,1,2,0:T(8,128)S(1)}, u32[]{:S(2)}, u32[]{:S(2)}) %collective-permute-start.2) | collective-permute-done | bytes 2208 | tf_op jit(solution)/shard_map/ppermute | solution.py:22
  47.1 4.1 %all-to-all-start.4 = ((f32[1,8,256]{2,0,1:T(1,128)}), f32[1,8,256]{2,0,1:T(1,128)S(1)}, u32[]{:S(2)}, u32[]{:S(2)}) async-start(f32[1,8,256]{2,0,1:T(1,128)} %bitcast.13), calls=%async_computation.4 | async-start | bytes 16384 | tf_op jit(solution)/shard_map/all_to_all | solution.py:68
  54.1 4.5 %collective-permute-start.8 = (f32[2,8,1,128]{3,1,2,0:T(8,128)S(1)}, f32[2,8,1,128]{3,1,2,0:T(8,128)S(1)}, u32[]{:S(2)}, u32[]{:S(2)}) collective-permute-start(f32[2,8,1,128]{3,1,2,0:T(8,128)S(1)} %get-tuple-element.45), channel_id=1, source_target_pairs={{0,1},{1,2},{2,3},{4,5},{5,6},{6,7},{8,9},{9,10},{10,11},{12,13},{... | collective-permute-start | bytes 24584 | tf_op jit(solution)/shard_map/ppermute | solution.py:22
  60.5 3.3 %all-to-all-start.5 = ((f32[1,8,256]{2,0,1:T(1,128)}), f32[1,8,256]{2,0,1:T(1,128)S(1)}, u32[]{:S(2)}, u32[]{:S(2)}) async-start(f32[1,8,256]{2,0,1:T(1,128)} %all_to_all.70), calls=%async_computation.5 | async-start | bytes 16384 | tf_op jit(solution)/shard_map/all_to_all | solution.py:72
  64.1 4.3 %all-to-all-done.5 = f32[1,8,256]{2,0,1:T(1,128)S(1)} async-done(((f32[1,8,256]{2,0,1:T(1,128)}), f32[1,8,256]{2,0,1:T(1,128)S(1)}, u32[]{:S(2)}, u32[]{:S(2)}) %all-to-all-start.5) | async-done | bytes 8224 | tf_op jit(solution)/shard_map/all_to_all | solution.py:72
  68.7 2.6 %collective-permute-start.11 = (f32[2,8,34,1]{3,1,2,0:T(8,128)S(1)}, f32[2,8,34,1]{3,1,2,0:T(8,128)S(1)}, u32[]{:S(2)}, u32[]{:S(2)}) collective-permute-start(f32[2,8,34,1]{3,1,2,0:T(8,128)S(1)} %get-tuple-element.37), channel_id=1, source_target_pairs={{4,0},{8,4},{12,8},{16,12},{20,16},{24,20},{28,24},{0,28},{5,1},{9... | collective-permute-start | bytes 6536 | tf_op jit(solution)/shard_map/ppermute | solution.py:23
  71.4 7.1 %collective-permute-done.10 = f32[2,8,34,1]{3,1,2,0:T(8,128)S(1)} collective-permute-done((f32[2,8,34,1]{3,1,2,0:T(8,128)S(1)}, f32[2,8,34,1]{3,1,2,0:T(8,128)S(1)}, u32[]{:S(2)}, u32[]{:S(2)}) %collective-permute-start.10) | collective-permute-done | bytes 2208 | tf_op jit(solution)/shard_map/ppermute | solution.py:22
  80.5 3.3 %all-to-all-start.6 = ((f32[1,8,256]{2,0,1:T(1,128)}), f32[1,8,256]{2,0,1:T(1,128)S(1)}, u32[]{:S(2)}, u32[]{:S(2)}) async-start(f32[1,8,256]{2,0,1:T(1,128)} %bitcast.19), calls=%async_computation.6 | async-start | bytes 16384 | tf_op jit(solution)/shard_map/all_to_all | solution.py:68
  83.8 4.6 %collective-permute-start.12 = (f32[2,8,1,128]{3,1,2,0:T(8,128)S(1)}, f32[2,8,1,128]{3,1,2,0:T(8,128)S(1)}, u32[]{:S(2)}, u32[]{:S(2)}) collective-permute-start(f32[2,8,1,128]{3,1,2,0:T(8,128)S(1)} %get-tuple-element.43), channel_id=1, source_target_pairs={{0,1},{1,2},{2,3},{4,5},{5,6},{6,7},{8,9},{9,10},{10,11},{12,13},{... | collective-permute-start | bytes 24584 | tf_op jit(solution)/shard_map/ppermute | solution.py:22
  90.3 4.1 %all-to-all-start.7 = ((f32[1,8,256]{2,0,1:T(1,128)}), f32[1,8,256]{2,0,1:T(1,128)S(1)}, u32[]{:S(2)}, u32[]{:S(2)}) async-start(f32[1,8,256]{2,0,1:T(1,128)} %all_to_all.74), calls=%async_computation.7 | async-start | bytes 16384 | tf_op jit(solution)/shard_map/all_to_all | solution.py:72
  94.4 4.7 %all-to-all-done.7 = f32[1,8,256]{2,0,1:T(1,128)S(1)} async-done(((f32[1,8,256]{2,0,1:T(1,128)}), f32[1,8,256]{2,0,1:T(1,128)S(1)}, u32[]{:S(2)}, u32[]{:S(2)}) %all-to-all-start.7) | async-done | bytes 8224 | tf_op jit(solution)/shard_map/all_to_all | solution.py:72
  102.0 7.2 %collective-permute-done.14 = f32[2,8,34,1]{3,1,2,0:T(8,128)S(1)} collective-permute-done((f32[2,8,34,1]{3,1,2,0:T(8,128)S(1)}, f32[2,8,34,1]{3,1,2,0:T(8,128)S(1)}, u32[]{:S(2)}, u32[]{:S(2)}) %collective-permute-start.14) | collective-permute-done | bytes 2208 | tf_op jit(solution)/shard_map/ppermute | solution.py:22
  110.8 3.3 %all-to-all-start.8 = ((f32[1,8,256]{2,0,1:T(1,128)}), f32[1,8,256]{2,0,1:T(1,128)S(1)}, u32[]{:S(2)}, u32[]{:S(2)}) async-start(f32[1,8,256]{2,0,1:T(1,128)} %bitcast.25), calls=%async_computation.8 | async-start | bytes 16384 | tf_op jit(solution)/shard_map/all_to_all | solution.py:68
  114.1 4.6 %collective-permute-start.16 = (f32[2,8,1,128]{3,1,2,0:T(8,128)S(1)}, f32[2,8,1,128]{3,1,2,0:T(8,128)S(1)}, u32[]{:S(2)}, u32[]{:S(2)}) collective-permute-start(f32[2,8,1,128]{3,1,2,0:T(8,128)S(1)} %get-tuple-element.41), channel_id=1, source_target_pairs={{0,1},{1,2},{2,3},{4,5},{5,6},{6,7},{8,9},{9,10},{10,11},{12,13},{... | collective-permute-start | bytes 24584 | tf_op jit(solution)/shard_map/ppermute | solution.py:22
  120.6 4.1 %all-to-all-start.9 = ((f32[1,8,256]{2,0,1:T(1,128)}), f32[1,8,256]{2,0,1:T(1,128)S(1)}, u32[]{:S(2)}, u32[]{:S(2)}) async-start(f32[1,8,256]{2,0,1:T(1,128)} %all_to_all.78), calls=%async_computation.9 | async-start | bytes 16384 | tf_op jit(solution)/shard_map/all_to_all | solution.py:72
  124.7 4.7 %all-to-all-done.9 = f32[1,8,256]{2,0,1:T(1,128)S(1)} async-done(((f32[1,8,256]{2,0,1:T(1,128)}), f32[1,8,256]{2,0,1:T(1,128)S(1)}, u32[]{:S(2)}, u32[]{:S(2)}) %all-to-all-start.9) | async-done | bytes 8224 | tf_op jit(solution)/shard_map/all_to_all | solution.py:72
  133.7 5.8 %collective-permute-done.18 = f32[2,8,34,1]{3,1,2,0:T(8,128)S(1)} collective-permute-done((f32[2,8,34,1]{3,1,2,0:T(8,128)S(1)}, f32[2,8,34,1]{3,1,2,0:T(8,128)S(1)}, u32[]{:S(2)}, u32[]{:S(2)}) %collective-permute-start.18) | collective-permute-done | bytes 2208 | tf_op jit(solution)/shard_map/ppermute | solution.py:22
  (98 shorter events, 36.6 us)
Async XLA Ops:
  2.5 9.9 %all-to-all-start = ((f32[1,8,256]{2,0,1:T(1,128)}), f32[1,8,256]{2,0,1:T(1,128)S(1)}, u32[]{:S(2)}, u32[]{:S(2)}) async-start(f32[1,8,256]{2,0,1:T(1,128)} %bitcast.2), calls=%async_computation | async-start | bytes 16384 | tf_op jit(solution)/shard_map/all_to_all | solution.py:68
  12.3 8.7 %all-to-all-start.2 = ((f32[1,8,128]{2,0,1:T(1,128)}), f32[1,8,128]{2,0,1:T(1,128)S(1)}, u32[]{:S(2)}, u32[]{:S(2)}) async-start(f32[1,8,128]{2,0,1:T(1,128)} %bitcast.7), calls=%async_computation.2 | async-start | bytes 8192 | tf_op jit(solution)/shard_map/all_to_all | solution.py:68
  15.6 20.2 %collective-permute-start = (f32[2,8,1,128]{3,1,2,0:T(8,128)S(1)}, f32[2,8,1,128]{3,1,2,0:T(8,128)S(1)}, u32[]{:S(2)}, u32[]{:S(2)}) collective-permute-start(f32[2,8,1,128]{3,1,2,0:T(8,128)S(1)} %get-tuple-element.47), channel_id=1, source_target_pairs={{0,1},{1,2},{2,3},{4,5},{5,6},{6,7},{8,9},{9,10},{10,11},{12,13},{... | collective-permute-start | bytes 24584 | tf_op jit(solution)/shard_map/ppermute | solution.py:22
  19.2 16.7 %collective-permute-start.1 = (f32[2,8,1,128]{3,1,2,0:T(8,128)S(1)}, f32[2,8,1,128]{3,1,2,0:T(8,128)S(1)}, u32[]{:S(2)}, u32[]{:S(2)}) collective-permute-start(f32[2,8,1,128]{3,1,2,0:T(8,128)S(1)} %get-tuple-element.46), channel_id=1, source_target_pairs={{1,0},{2,1},{3,2},{5,4},{6,5},{7,6},{9,8},{10,9},{11,10},{13,12},{... | collective-permute-start | bytes 24584 | tf_op jit(solution)/shard_map/ppermute | solution.py:23
  21.1 10.5 %all-to-all-start.1 = ((f32[1,8,256]{2,0,1:T(1,128)}), f32[1,8,256]{2,0,1:T(1,128)S(1)}, u32[]{:S(2)}, u32[]{:S(2)}) async-start(f32[1,8,256]{2,0,1:T(1,128)} %all_to_all.62), calls=%async_computation.1 | async-start | bytes 16384 | tf_op jit(solution)/shard_map/all_to_all | solution.py:72
  25.2 13.6 %collective-permute-start.4 = (f32[1,8,1,128]{3,1,2,0:T(8,128)S(1)}, f32[1,8,1,128]{3,1,2,0:T(8,128)S(1)}, u32[]{:S(2)}, u32[]{:S(2)}) collective-permute-start(f32[1,8,1,128]{3,1,2,0:T(8,128)S(1)} %get-tuple-element.51), channel_id=1, source_target_pairs={{0,1},{1,2},{2,3},{4,5},{5,6},{6,7},{8,9},{9,10},{10,11},{12,13},{... | collective-permute-start | bytes 12296 | tf_op jit(solution)/shard_map/ppermute | solution.py:22
  29.7 9.1 %collective-permute-start.5 = (f32[1,8,1,128]{3,1,2,0:T(8,128)S(1)}, f32[1,8,1,128]{3,1,2,0:T(8,128)S(1)}, u32[]{:S(2)}, u32[]{:S(2)}) collective-permute-start(f32[1,8,1,128]{3,1,2,0:T(8,128)S(1)} %get-tuple-element.50), channel_id=1, source_target_pairs={{1,0},{2,1},{3,2},{5,4},{6,5},{7,6},{9,8},{10,9},{11,10},{13,12},{... | collective-permute-start | bytes 12296 | tf_op jit(solution)/shard_map/ppermute | solution.py:23
  31.6 8.8 %all-to-all-start.3 = ((f32[1,8,128]{2,0,1:T(1,128)}), f32[1,8,128]{2,0,1:T(1,128)S(1)}, u32[]{:S(2)}, u32[]{:S(2)}) async-start(f32[1,8,128]{2,0,1:T(1,128)} %all_to_all.66), calls=%async_computation.3 | async-start | bytes 8192 | tf_op jit(solution)/shard_map/all_to_all | solution.py:72
  47.1 12.8 %all-to-all-start.4 = ((f32[1,8,256]{2,0,1:T(1,128)}), f32[1,8,256]{2,0,1:T(1,128)S(1)}, u32[]{:S(2)}, u32[]{:S(2)}) async-start(f32[1,8,256]{2,0,1:T(1,128)} %bitcast.13), calls=%async_computation.4 | async-start | bytes 16384 | tf_op jit(solution)/shard_map/all_to_all | solution.py:68
  51.3 12.6 %collective-permute-start.6 = (f32[1,8,34,1]{3,1,2,0:T(8,128)S(1)}, f32[1,8,34,1]{3,1,2,0:T(8,128)S(1)}, u32[]{:S(2)}, u32[]{:S(2)}) collective-permute-start(f32[1,8,34,1]{3,1,2,0:T(8,128)S(1)} %get-tuple-element.48), channel_id=1, source_target_pairs={{0,4},{4,8},{8,12},{12,16},{16,20},{20,24},{24,28},{28,0},{1,5},{5... | collective-permute-start | bytes 3272 | tf_op jit(solution)/shard_map/ppermute | solution.py:22
  52.3 11.6 %collective-permute-start.7 = (f32[1,8,34,1]{3,1,2,0:T(8,128)S(1)}, f32[1,8,34,1]{3,1,2,0:T(8,128)S(1)}, u32[]{:S(2)}, u32[]{:S(2)}) collective-permute-start(f32[1,8,34,1]{3,1,2,0:T(8,128)S(1)} %get-tuple-element.49), channel_id=1, source_target_pairs={{4,0},{8,4},{12,8},{16,12},{20,16},{24,20},{28,24},{0,28},{5,1},{9... | collective-permute-start | bytes 3272 | tf_op jit(solution)/shard_map/ppermute | solution.py:23
  54.1 10.0 %collective-permute-start.8 = (f32[2,8,1,128]{3,1,2,0:T(8,128)S(1)}, f32[2,8,1,128]{3,1,2,0:T(8,128)S(1)}, u32[]{:S(2)}, u32[]{:S(2)}) collective-permute-start(f32[2,8,1,128]{3,1,2,0:T(8,128)S(1)} %get-tuple-element.45), channel_id=1, source_target_pairs={{0,1},{1,2},{2,3},{4,5},{5,6},{6,7},{8,9},{9,10},{10,11},{12,13},{... | collective-permute-start | bytes 24584 | tf_op jit(solution)/shard_map/ppermute | solution.py:22
  68.7 9.9 %collective-permute-start.10 = (f32[2,8,34,1]{3,1,2,0:T(8,128)S(1)}, f32[2,8,34,1]{3,1,2,0:T(8,128)S(1)}, u32[]{:S(2)}, u32[]{:S(2)}) collective-permute-start(f32[2,8,34,1]{3,1,2,0:T(8,128)S(1)} %get-tuple-element.36), channel_id=1, source_target_pairs={{0,4},{4,8},{8,12},{12,16},{16,20},{20,24},{24,28},{28,0},{1,5},{5... | collective-permute-start | bytes 6536 | tf_op jit(solution)/shard_map/ppermute | solution.py:22
  68.7 9.8 %collective-permute-start.11 = (f32[2,8,34,1]{3,1,2,0:T(8,128)S(1)}, f32[2,8,34,1]{3,1,2,0:T(8,128)S(1)}, u32[]{:S(2)}, u32[]{:S(2)}) collective-permute-start(f32[2,8,34,1]{3,1,2,0:T(8,128)S(1)} %get-tuple-element.37), channel_id=1, source_target_pairs={{4,0},{8,4},{12,8},{16,12},{20,16},{24,20},{28,24},{0,28},{5,1},{9... | collective-permute-start | bytes 6536 | tf_op jit(solution)/shard_map/ppermute | solution.py:23
  80.5 9.2 %all-to-all-start.6 = ((f32[1,8,256]{2,0,1:T(1,128)}), f32[1,8,256]{2,0,1:T(1,128)S(1)}, u32[]{:S(2)}, u32[]{:S(2)}) async-start(f32[1,8,256]{2,0,1:T(1,128)} %bitcast.19), calls=%async_computation.6 | async-start | bytes 16384 | tf_op jit(solution)/shard_map/all_to_all | solution.py:68
  83.8 10.6 %collective-permute-start.12 = (f32[2,8,1,128]{3,1,2,0:T(8,128)S(1)}, f32[2,8,1,128]{3,1,2,0:T(8,128)S(1)}, u32[]{:S(2)}, u32[]{:S(2)}) collective-permute-start(f32[2,8,1,128]{3,1,2,0:T(8,128)S(1)} %get-tuple-element.43), channel_id=1, source_target_pairs={{0,1},{1,2},{2,3},{4,5},{5,6},{6,7},{8,9},{9,10},{10,11},{12,13},{... | collective-permute-start | bytes 24584 | tf_op jit(solution)/shard_map/ppermute | solution.py:22
  90.3 8.8 %all-to-all-start.7 = ((f32[1,8,256]{2,0,1:T(1,128)}), f32[1,8,256]{2,0,1:T(1,128)S(1)}, u32[]{:S(2)}, u32[]{:S(2)}) async-start(f32[1,8,256]{2,0,1:T(1,128)} %all_to_all.74), calls=%async_computation.7 | async-start | bytes 16384 | tf_op jit(solution)/shard_map/all_to_all | solution.py:72
  99.3 9.9 %collective-permute-start.14 = (f32[2,8,34,1]{3,1,2,0:T(8,128)S(1)}, f32[2,8,34,1]{3,1,2,0:T(8,128)S(1)}, u32[]{:S(2)}, u32[]{:S(2)}) collective-permute-start(f32[2,8,34,1]{3,1,2,0:T(8,128)S(1)} %get-tuple-element.32), channel_id=1, source_target_pairs={{0,4},{4,8},{8,12},{12,16},{16,20},{20,24},{24,28},{28,0},{1,5},{5... | collective-permute-start | bytes 6536 | tf_op jit(solution)/shard_map/ppermute | solution.py:22
  99.3 9.8 %collective-permute-start.15 = (f32[2,8,34,1]{3,1,2,0:T(8,128)S(1)}, f32[2,8,34,1]{3,1,2,0:T(8,128)S(1)}, u32[]{:S(2)}, u32[]{:S(2)}) collective-permute-start(f32[2,8,34,1]{3,1,2,0:T(8,128)S(1)} %get-tuple-element.33), channel_id=1, source_target_pairs={{4,0},{8,4},{12,8},{16,12},{20,16},{24,20},{28,24},{0,28},{5,1},{9... | collective-permute-start | bytes 6536 | tf_op jit(solution)/shard_map/ppermute | solution.py:23
  110.8 9.2 %all-to-all-start.8 = ((f32[1,8,256]{2,0,1:T(1,128)}), f32[1,8,256]{2,0,1:T(1,128)S(1)}, u32[]{:S(2)}, u32[]{:S(2)}) async-start(f32[1,8,256]{2,0,1:T(1,128)} %bitcast.25), calls=%async_computation.8 | async-start | bytes 16384 | tf_op jit(solution)/shard_map/all_to_all | solution.py:68
  114.1 10.6 %collective-permute-start.16 = (f32[2,8,1,128]{3,1,2,0:T(8,128)S(1)}, f32[2,8,1,128]{3,1,2,0:T(8,128)S(1)}, u32[]{:S(2)}, u32[]{:S(2)}) collective-permute-start(f32[2,8,1,128]{3,1,2,0:T(8,128)S(1)} %get-tuple-element.41), channel_id=1, source_target_pairs={{0,1},{1,2},{2,3},{4,5},{5,6},{6,7},{8,9},{9,10},{10,11},{12,13},{... | collective-permute-start | bytes 24584 | tf_op jit(solution)/shard_map/ppermute | solution.py:22
  120.6 8.8 %all-to-all-start.9 = ((f32[1,8,256]{2,0,1:T(1,128)}), f32[1,8,256]{2,0,1:T(1,128)S(1)}, u32[]{:S(2)}, u32[]{:S(2)}) async-start(f32[1,8,256]{2,0,1:T(1,128)} %all_to_all.78), calls=%async_computation.9 | async-start | bytes 16384 | tf_op jit(solution)/shard_map/all_to_all | solution.py:72
  129.6 9.9 %collective-permute-start.18 = (f32[2,8,34,1]{3,1,2,0:T(8,128)S(1)}, f32[2,8,34,1]{3,1,2,0:T(8,128)S(1)}, u32[]{:S(2)}, u32[]{:S(2)}) collective-permute-start(f32[2,8,34,1]{3,1,2,0:T(8,128)S(1)} %get-tuple-element.30), channel_id=1, source_target_pairs={{0,4},{4,8},{8,12},{12,16},{16,20},{20,24},{24,28},{28,0},{1,5},{5... | collective-permute-start | bytes 6536 | tf_op jit(solution)/shard_map/ppermute | solution.py:22
  129.7 9.8 %collective-permute-start.19 = (f32[2,8,34,1]{3,1,2,0:T(8,128)S(1)}, f32[2,8,34,1]{3,1,2,0:T(8,128)S(1)}, u32[]{:S(2)}, u32[]{:S(2)}) collective-permute-start(f32[2,8,34,1]{3,1,2,0:T(8,128)S(1)} %get-tuple-element.31), channel_id=1, source_target_pairs={{4,0},{8,4},{12,8},{16,12},{20,16},{24,20},{28,24},{0,28},{5,1},{9... | collective-permute-start | bytes 6536 | tf_op jit(solution)/shard_map/ppermute | solution.py:23
  (9 other events, 48.9 us)
where the time goes:
time: 143 us; the launch traced here: 142 us
  starting transfers between devices  80.9 us (57%)
  waiting for transfers between devices  43.6 us (30%)
  local copies, waits for them, and re-layouts  10.7 us (7%)
  other arithmetic  5.8 us (4%)
    ppermute x10, starting transfers between devices, with_halo(): before = lax.ppermute(last, axis, up)  23.5 us
    ppermute x10, waiting for transfers between devices, with_halo(): before = lax.ppermute(last, axis, up)  23.3 us
    all_to_all x5, starting transfers between devices, mirror_partner(): lax.all_to_all(turned, 'lon', split_axis=1, concat_axis=1, tiled=True)  19.8 us
    all_to_all x5, starting transfers between devices, mirror_partner(): lax.all_to_all(flat, 'lon', split_axis=1, concat_axis=1, tiled=True)  19.2 us
    ppermute x10, starting transfers between devices, with_halo(): after = lax.ppermute(first, axis, down)  18.4 us
    all_to_all x5, waiting for transfers between devices, mirror_partner(): lax.all_to_all(turned, 'lon', split_axis=1, concat_axis=1, tiled=True)  15.3 us
    all_to_all x5, waiting for transfers between devices, mirror_partner(): lax.all_to_all(flat, 'lon', split_axis=1, concat_axis=1, tiled=True)  3.95 us
    unnamed x10, local copies, waits for them, and re-layouts  3.65 us
  transfers between devices with their start and end apart: 30, of which 11 were waited for; matrix products, arithmetic and copies ran while one was open for 2% of the time, Pallas kernels for 0%

commit v1 on v0

v1 whole, which is shorter than its diff:
```python
import functools

import jax
import jax.numpy as jnp
from jax import lax
from jax.experimental import pallas as pl
from jax.experimental.pallas import tpu as pltpu
from jax.sharding import PartitionSpec as P

STEPS = 2
TIME_STEP = 0.8
DIFFUSIVITY = 0.15
PRESSURE_GAIN = 0.12
LAYER_DEPTH = 0.5
HALO = 2 * STEPS
FIELDS = 5
MESH = pl.DeviceIdType.MESH


def lane_iota(shape):
    return lax.broadcasted_iota(jnp.int32, shape, len(shape) - 1)


def swap_lanes(x, bits):
    width = x.shape[-1]
    lane = lane_iota(x.shape)
    bit = 1
    while bit < width:
        if bits & bit:
            up = pltpu.roll(x, bit, x.ndim - 1)
            if 2 * bit == width:
                x = up
            else:
                x = jnp.where((lane & bit) != 0, up, pltpu.roll(x, width - bit, x.ndim - 1))
        bit *= 2
    return x


def blocks(first, count, size, body):
    number = (count + size - 1) // size

    def step(b, _):
        start = jnp.minimum(first + b * size, first + count - size)
        body(start)
        return 0

    lax.fori_loop(0, number, step, 0)


def pressure_pass(temp, salt, load, first, count, size):
    def body(start):
        rows = pl.ds(start, size)
        total = (0.8 * LAYER_DEPTH) * salt[rows] - (0.2 * LAYER_DEPTH) * temp[rows]
        level = lax.broadcasted_iota(jnp.int32, total.shape, 1)
        shift = 1
        while shift < total.shape[1]:
            total = total + jnp.where(level >= shift, pltpu.roll(total, shift, 1), 0.0)
            shift *= 2
        load[rows] = total

    blocks(first, count, size, body)


def velocity_pass(load, wet, east, north, east_to, north_to, first, count, size):
    def body(start):
        rows = pl.ds(start, size)
        here = load[rows]
        width = here.shape[2]
        sea = wet[rows]
        grad_east = pltpu.roll(here, width - 1, 2) - pltpu.roll(here, 1, 2)
        grad_north = load[pl.ds(start + 1, size)] - load[pl.ds(start - 1, size)]
        east_to[rows] = (east[rows] - PRESSURE_GAIN * grad_east) * sea
        north_to[rows] = (north[rows] - PRESSURE_GAIN * grad_north) * sea

    blocks(first, count, size, body)


def tracer_pass(tracers, wet, east, north, tracers_to, first, count, size):
    def body(start):
        rows = pl.ds(start, size)
        around = pl.ds(start - 1, size + 2)
        sea = wet[around]
        inner = sea[1:-1]
        width = sea.shape[2]
        flow = east[rows]
        both = inner * pltpu.roll(inner, width - 1, 2)
        mean = 0.25 * (flow + pltpu.roll(flow, width - 1, 2))
        east_here, east_next = (mean + DIFFUSIVITY) * both, (mean - DIFFUSIVITY) * both
        rise = north[around]
        both = sea[:-1] * sea[1:]
        mean = 0.25 * (rise[:-1] + rise[1:])
        north_here, north_next = (mean + DIFFUSIVITY) * both, (mean - DIFFUSIVITY) * both
        scale = TIME_STEP * inner
        for tracer, tracer_to in zip(tracers, tracers_to):
            q = tracer[around]
            mid = q[1:-1]
            flux_east = east_here * mid + east_next * pltpu.roll(mid, width - 1, 2)
            flux_north = north_here * q[:-1] + north_next * q[1:]
            spread = flux_east - pltpu.roll(flux_east, 1, 2) + (flux_north[1:] - flux_north[:-1])
            tracer_to[rows] = mid - scale * spread

    blocks(first, count, size, body)


def run_steps(ext, work, rows, size):
    every = rows + 2 * HALO
    load = work.at[0]
    wet = ext.at[4]
    held = [ext.at[f] for f in range(4)]
    for step in range(STEPS):
        to = [work.at[1 + 4 * step + f] for f in range(4)]
        edge = 2 * step
        pressure_pass(held[0], held[1], load, edge, every - 2 * edge, size)
        velocity_pass(load, wet, held[2], held[3], to[2], to[3], edge + 1, every - 2 * edge - 2, size)
        tracer_pass(held[:2], wet, to[2], to[3], to[:2], edge + 2, every - 2 * edge - 4, size)
        held = to


def kernel(
    rows,
    levels,
    temp_hbm,
    salt_hbm,
    east_hbm,
    north_hbm,
    wet_hbm,
    temp_out,
    salt_out,
    east_out,
    north_out,
    staged,
    staged_wet,
    ext,
    seam,
    main_work,
    seam_work,
    packed,
    from_left,
    from_right,
    merged,
    corner,
    load_sem,
    row_send,
    row_recv,
    col_send,
    col_recv,
    corner_send,
    corner_recv,
):
    lon, lat = lax.axis_index("lon"), lax.axis_index("lat")
    lon_total, lat_total = lax.axis_size("lon"), lax.axis_size("lat")
    at_top = lat == lat_total - 1
    has_south = lat > 0
    left, right = lax.rem(lon + lon_total - 1, lon_total), lax.rem(lon + 1, lon_total)
    top = (lat // (lat_total - 1)) if lat_total > 1 else 1
    north_lon = lon + top * (lon_total - 1 - 2 * lon)
    north_lat = lat + 1 - top
    north_id = {"lon": north_lon, "lat": north_lat}
    south_id = {"lon": lon, "lat": lat - 1}
    left_id, right_id = {"lon": left, "lat": lat}, {"lon": right, "lat": lat}

    inputs = (temp_hbm, salt_hbm, east_hbm, north_hbm)
    loads = [pltpu.make_async_copy(h, staged.at[f], load_sem.at[f]) for f, h in enumerate(inputs)]
    loads.append(pltpu.make_async_copy(wet_hbm, staged_wet, load_sem.at[4]))
    for copy in loads:
        copy.start()

    barrier = pltpu.get_barrier_semaphore()
    for other in (left_id, right_id, north_id):
        pl.semaphore_signal(barrier, inc=1, device_id=other, device_id_type=MESH)

    @pl.when(has_south)
    def _():
        pl.semaphore_signal(barrier, inc=1, device_id=south_id, device_id_type=MESH)

    for f in range(FIELDS):
        loads[f].wait()
        for r in range(rows):
            if f < 4:
                value = staged[f, pl.ds(r, levels, stride=rows), :]
            else:
                value = staged_wet[pl.ds(r, levels, stride=rows), :].astype(jnp.float32)
            ext[f, HALO + r] = value

    pl.semaphore_wait(barrier, 3 + jnp.minimum(lat, 1))

    north_base = HALO + rows
    row_north = pltpu.make_async_remote_copy(
        src_ref=ext.at[:, pl.ds(rows, HALO)],
        dst_ref=ext.at[:, pl.ds(top * north_base, HALO)],
        send_sem=row_send.at[0],
        recv_sem=row_recv.at[top],
        device_id=north_id,
        device_id_type=MESH,
    )
    row_south = pltpu.make_async_remote_copy(
        src_ref=ext.at[:, pl.ds(HALO, HALO)],
        dst_ref=ext.at[:, pl.ds(north_base, HALO)],
        send_sem=row_send.at[1],
        recv_sem=row_recv.at[1],
        device_id=south_id,
        device_id_type=MESH,
    )
    row_north.start()

    @pl.when(has_south)
    def _():
        row_south.start()

    width = ext.shape[-1]
    slot_lanes = 2 * HALO
    groups = rows // HALO
    gathered = jnp.zeros((groups, levels, width), jnp.float32)
    slot_of = lane_iota(gathered.shape) // slot_lanes
    for f in range(4):
        block = ext[f, HALO : HALO + rows].reshape(groups, HALO, levels, width)
        for i in range(HALO):
            slot = HALO * f + i
            turned = pltpu.roll(block[:, i], (HALO + slot_lanes * slot) % width, 2)
            gathered = jnp.where(slot_of == slot, turned, gathered)
    packed[1 : 1 + groups] = gathered
    slots = width // slot_lanes
    halves = jnp.zeros((2, levels, width), jnp.float32)
    slot_of = lane_iota(halves.shape) // slot_lanes
    block = ext[4, HALO : HALO + rows].reshape(2, slots, levels, width)
    for slot in range(slots):
        turned = pltpu.roll(block[:, slot], (HALO + slot_lanes * slot) % width, 2)
        halves = jnp.where(slot_of == slot, turned, halves)
    packed[0] = halves[0]
    packed[1 + groups] = halves[1]

    to_left = pltpu.make_async_remote_copy(
        src_ref=packed,
        dst_ref=from_right,
        send_sem=col_send.at[0],
        recv_sem=col_recv.at[1],
        device_id=left_id,
        device_id_type=MESH,
    )
    to_right = pltpu.make_async_remote_copy(
        src_ref=packed,
        dst_ref=from_left,
        send_sem=col_send.at[1],
        recv_sem=col_recv.at[0],
        device_id=right_id,
        device_id_type=MESH,
    )
    to_left.start()
    to_right.start()

    @pl.when(lat == 0)
    def _():
        ext[:, 0:HALO] = jnp.zeros((FIELDS, HALO, levels, width), jnp.float32)
        corner[0] = jnp.zeros((2, levels, width), jnp.float32)

    to_left.wait_recv()
    to_right.wait_recv()
    before, after = from_left[...], from_right[...]
    lane = lane_iota(before.shape)
    merged[...] = jnp.where(
        (lane & HALO) != 0, pltpu.roll(before, HALO, 2), pltpu.roll(after, width - HALO, 2)
    )

    corner_north = pltpu.make_async_remote_copy(
        src_ref=merged.at[pl.ds(groups, 2)],
        dst_ref=corner.at[top],
        send_sem=corner_send.at[0],
        recv_sem=corner_recv.at[top],
        device_id=north_id,
        device_id_type=MESH,
    )
    corner_south = pltpu.make_async_remote_copy(
        src_ref=merged.at[pl.ds(0, 2)],
        dst_ref=corner.at[1],
        send_sem=corner_send.at[1],
        recv_sem=corner_recv.at[1],
        device_id=south_id,
        device_id_type=MESH,
    )
    corner_north.start()

    @pl.when(has_south)
    def _():
        corner_south.start()

    row_south.wait_recv()

    @pl.when(has_south)
    def _():
        pltpu.make_async_remote_copy(
            src_ref=ext.at[:, pl.ds(rows, HALO)],
            dst_ref=ext.at[:, pl.ds(0, HALO)],
            send_sem=row_send.at[0],
            recv_sem=row_recv.at[0],
            device_id=north_id,
            device_id_type=MESH,
        ).wait_recv()

    @pl.when(at_top)
    def _():
        for f in range(FIELDS):
            turned = swap_lanes(ext[f, north_base : north_base + HALO], width - 1)
            if f in (2, 3):
                turned = -turned
            for i in range(HALO):
                ext[f, north_base + i] = turned[HALO - 1 - i]

    run_steps(ext, main_work, rows, 4)

    def stitch(own, piece, slot):
        spot = lane_iota(own.shape)
        edges = pltpu.roll(piece, (width - slot_lanes * (slot + 1)) % width, own.ndim - 1)
        value = jnp.where(spot < width // 2, own, pltpu.roll(own, width - slot_lanes, own.ndim - 1))
        return jnp.where(spot >= width - slot_lanes, edges, value)

    center = merged[1 : 1 + groups]
    for f in range(4):
        block = ext[f, HALO : HALO + rows].reshape(groups, HALO, levels, width)
        for i in range(HALO):
            value = stitch(block[:, i], center, HALO * f + i)
            for g in range(groups):
                seam[f, HALO + HALO * g + i] = value[g]
    for half in range(2):
        piece = merged[half * (1 + groups)]
        for slot in range(slots):
            r = HALO + slots * half + slot
            seam[4, r] = stitch(ext[4, r], piece, slot)

    corner_south.wait_recv()

    @pl.when(has_south)
    def _():
        pltpu.make_async_remote_copy(
            src_ref=merged.at[pl.ds(groups, 2)],
            dst_ref=corner.at[0],
            send_sem=corner_send.at[0],
            recv_sem=corner_recv.at[0],
            device_id=north_id,
            device_id_type=MESH,
        ).wait_recv()

    @pl.when(at_top)
    def _():
        fields = swap_lanes(corner[1, 0], slot_lanes * HALO - 1)
        fields = jnp.where(lane_iota(fields.shape) >= width // 2, -fields, fields)
        sea = swap_lanes(corner[1, 1], width - 1)
        corner[1, 0] = sea
        corner[1, 1] = fields

    for side in range(2):
        fields, sea = corner[side, side], corner[side, 1 - side]
        base = side * north_base
        for i in range(HALO):
            for f in range(4):
                seam[f, base + i] = stitch(ext[f, base + i], fields, HALO * f + i)
            slot = i if side else slots - HALO + i
            seam[4, base + i] = stitch(ext[4, base + i], sea, slot)

    run_steps(seam, seam_work, rows, 4)

    for f, out in enumerate((temp_out, salt_out, east_out, north_out)):
        for r in range(rows):
            edge = seam_work[5 + f, HALO + r]
            spot = lane_iota(edge.shape)
            value = main_work[5 + f, HALO + r]
            value = jnp.where(spot < HALO, edge, value)
            value = jnp.where(spot >= width - HALO, pltpu.roll(edge, slot_lanes, 1), value)
            out[pl.ds(r, levels, stride=rows), :] = value

    row_north.wait_send()
    to_left.wait_send()
    to_right.wait_send()
    corner_north.wait_send()

    @pl.when(has_south)
    def _():
        row_south.wait_send()
        corner_south.wait_send()


def shards(temp, salt, east, north, wet):
    levels, rows, columns = temp.shape
    flat = [x.reshape(levels * rows, columns) for x in (temp, salt, east, north, wet)]
    every = rows + 2 * HALO
    pieces = rows // HALO + 2
    plane = (levels, columns)
    vmem = lambda *lead: pltpu.VMEM(lead + plane, jnp.float32)
    outs = pl.pallas_call(
        functools.partial(kernel, rows, levels),
        out_shape=[jax.ShapeDtypeStruct((levels * rows, columns), jnp.float32)] * 4,
        in_specs=[pl.BlockSpec(memory_space=pl.ANY)] * 5,
        out_specs=[pl.BlockSpec(memory_space=pltpu.VMEM)] * 4,
        scratch_shapes=[
            pltpu.VMEM((4, levels * rows, columns), jnp.float32),
            pltpu.VMEM((levels * rows, columns), jnp.int32),
            vmem(FIELDS, every),
            vmem(FIELDS, every),
            vmem(9, every),
            vmem(9, every),
            vmem(pieces),
            vmem(pieces),
            vmem(pieces),
            vmem(pieces),
            vmem(2, 2),
            pltpu.SemaphoreType.DMA((FIELDS,)),
            pltpu.SemaphoreType.DMA((2,)),
            pltpu.SemaphoreType.DMA((2,)),
            pltpu.SemaphoreType.DMA((2,)),
            pltpu.SemaphoreType.DMA((2,)),
            pltpu.SemaphoreType.DMA((2,)),
            pltpu.SemaphoreType.DMA((2,)),
        ],
        compiler_params=pltpu.CompilerParams(
            collective_id=0, has_side_effects=True, vmem_limit_bytes=60 * 1024 * 1024
        ),
    )(*flat)
    return tuple(x.reshape(levels, rows, columns) for x in outs)


def solution(mesh):
    spec = P(None, "lat", "lon")
    return jax.shard_map(
        shards, mesh=mesh, in_specs=(spec,) * 5, out_specs=(spec,) * 4, check_vma=False
    )
```

time: 143 us -> 25.9 us (0.18)
  the two profiles are of different devices: /device:TPU:0 before, /device:TPU:25 now
where the time goes in v1:
time: 25.9 us; the launch traced here: 25.7 us
  Pallas kernels  20.8 us (80%)
  local copies, waits for them, and re-layouts  4.16 us (16%)
  between operations  0.65 us (3%)
    pallas_call x1, Pallas kernels, shards(): pl.pallas_call(functools.partial(kernel, rows, levels), out_shape=[jax.Sh...  20.8 us
    unnamed x10, local copies, waits for them, and re-layouts  4.16 us

profile of v1, /device:TPU:25, one launch (start us, length us, event | category | flops | bytes accessed | tf_op | source)
XLA Modules:
  0.0 25.7 jit_solution(14292099020141780167)
XLA Ops:
  0.6 20.8 %shard_map.84 = (f32[256,128]{1,0:T(8,128)}, f32[256,128]{1,0:T(8,128)}, f32[256,128]{1,0:T(8,128)}, f32[256,128]{1,0:T(8,128)}) custom-call(f32[256,128]{1,0:T(8,128)} %bitcast.9, f32[256,128]{1,0:T(8,128)} %bitcast.10, f32[256,128]{1,0:T(8,128)} %bitcast.11, f32[256,128]{1,0:T(8,128)} %bitcast.12, s32[256,128]{1,0:T(8,128)} %bitcast.13), custom_call_target="tpu_custom_call" | custom-call | tf_op jit(solution)/shard_map/pallas_call | solution.py:388
  21.5 0.0 copy-start.2
  21.5 1.6 %copy.13 = f32[8,32,128]{2,1,0:T(8,128)} copy(f32[8,32,128]{2,1,0:T(8,128)} %bitcast.17) | data formatting | bytes 262144
  23.1 0.0 copy-done.2
  23.1 0.0 copy-start.1
  23.1 0.7 %copy.14 = f32[8,32,128]{2,1,0:T(8,128)} copy(f32[8,32,128]{2,1,0:T(8,128)S(1)} %bitcast.16) | data formatting | bytes 262144
  23.8 0.3 %copy-done.1 = f32[256,128]{1,0:T(8,128)S(1)} copy-done((f32[256,128]{1,0:T(8,128)S(1)}, f32[256,128]{1,0:T(8,128)}, u32[]{:S(2)}) %copy-start.1) | copy-done | bytes 131096
  24.1 0.0 copy-start
  24.1 0.7 %copy.15 = f32[8,32,128]{2,1,0:T(8,128)} copy(f32[8,32,128]{2,1,0:T(8,128)S(1)} %bitcast.15) | data formatting | bytes 262144
  24.7 0.3 %copy-done = f32[256,128]{1,0:T(8,128)S(1)} copy-done((f32[256,128]{1,0:T(8,128)S(1)}, f32[256,128]{1,0:T(8,128)}, u32[]{:S(2)}) %copy-start) | copy-done | bytes 131096
  25.0 0.7 %copy.16 = f32[8,32,128]{2,1,0:T(8,128)} copy(f32[8,32,128]{2,1,0:T(8,128)S(1)} %bitcast.14) | data formatting | bytes 262144
Async XLA Ops:
  21.5 1.6 %copy-start.2 = (f32[256,128]{1,0:T(8,128)S(1)}, f32[256,128]{1,0:T(8,128)}, u32[]{:S(2)}) copy-start(f32[256,128]{1,0:T(8,128)} %get-tuple-element.9) | copy-start | bytes 393220
  23.1 1.0 %copy-start.1 = (f32[256,128]{1,0:T(8,128)S(1)}, f32[256,128]{1,0:T(8,128)}, u32[]{:S(2)}) copy-start(f32[256,128]{1,0:T(8,128)} %get-tuple-element.10) | copy-start | bytes 393220
  24.1 1.0 %copy-start = (f32[256,128]{1,0:T(8,128)S(1)}, f32[256,128]{1,0:T(8,128)}, u32[]{:S(2)}) copy-start(f32[256,128]{1,0:T(8,128)} %get-tuple-element.11) | copy-start | bytes 393220

commit v2 on v1

--- a/solution.py
+++ b/solution.py
@@ -39,12 +39,8 @@
 def blocks(first, count, size, body):
     number = (count + size - 1) // size
 
-    def step(b, _):
-        start = jnp.minimum(first + b * size, first + count - size)
-        body(start)
-        return 0
-
-    lax.fori_loop(0, number, step, 0)
+    for b in range(number):
+        body(min(first + b * size, first + count - size))
 
 
 def pressure_pass(temp, salt, load, first, count, size):
@@ -305,7 +301,7 @@
             for i in range(HALO):
                 ext[f, north_base + i] = turned[HALO - 1 - i]
 
-    run_steps(ext, main_work, rows, 4)
+    run_steps(ext, main_work, rows, 8)
 
     def stitch(own, piece, slot):
         spot = lane_iota(own.shape)
@@ -356,7 +352,7 @@
             slot = i if side else slots - HALO + i
             seam[4, base + i] = stitch(ext[4, base + i], sea, slot)
 
-    run_steps(seam, seam_work, rows, 4)
+    run_steps(seam, seam_work, rows, 8)
 
     for f, out in enumerate((temp_out, salt_out, east_out, north_out)):
         for r in range(rows):
@@ -378,6 +374,18 @@
         corner_south.wait_send()
 
 
+def write_out(*refs):
+    count = (len(refs) - 1) // 2
+    sems = refs[-1]
+    copies = [
+        pltpu.make_async_copy(refs[f], refs[count + f], sems.at[f]) for f in range(count)
+    ]
+    for copy in copies:
+        copy.start()
+    for copy in copies:
+        copy.wait()
+
+
 def shards(temp, salt, east, north, wet):
     levels, rows, columns = temp.shape
     flat = [x.reshape(levels * rows, columns) for x in (temp, salt, east, north, wet)]
@@ -385,10 +393,11 @@
     pieces = rows // HALO + 2
     plane = (levels, columns)
     vmem = lambda *lead: pltpu.VMEM(lead + plane, jnp.float32)
+    flat = [pltpu.with_memory_space_constraint(x, pltpu.HBM) for x in flat]
     outs = pl.pallas_call(
         functools.partial(kernel, rows, levels),
-        out_shape=[jax.ShapeDtypeStruct((levels * rows, columns), jnp.float32)] * 4,
-        in_specs=[pl.BlockSpec(memory_space=pl.ANY)] * 5,
+        out_shape=[pltpu.VMEM((levels * rows, columns), jnp.float32)] * 4,
+        in_specs=[pl.BlockSpec(memory_space=pltpu.HBM)] * 5,
         out_specs=[pl.BlockSpec(memory_space=pltpu.VMEM)] * 4,
         scratch_shapes=[
             pltpu.VMEM((4, levels * rows, columns), jnp.float32),
@@ -411,9 +420,17 @@
             pltpu.SemaphoreType.DMA((2,)),
         ],
         compiler_params=pltpu.CompilerParams(
-            collective_id=0, has_side_effects=True, vmem_limit_bytes=60 * 1024 * 1024
+            collective_id=0, has_side_effects=True, vmem_limit_bytes=16 * 1024 * 1024
         ),
     )(*flat)
+    outs = pl.pallas_call(
+        write_out,
+        out_shape=[jax.ShapeDtypeStruct((levels * rows, columns), jnp.float32)] * 4,
+        in_specs=[pl.BlockSpec(memory_space=pltpu.VMEM)] * 4,
+        out_specs=[pl.BlockSpec(memory_space=pltpu.HBM)] * 4,
+        scratch_shapes=[pltpu.SemaphoreType.DMA((4,))],
+        compiler_params=pltpu.CompilerParams(vmem_limit_bytes=2 * 1024 * 1024),
+    )(*outs)
     return tuple(x.reshape(levels, rows, columns) for x in outs)
 
 

time: 25.9 us -> 14.3 us (0.55)
  the two profiles are of different devices: /device:TPU:25 before, /device:TPU:24 now
where the time goes in v2:
time: 14.3 us; the launch traced here: 14.2 us
  Pallas kernels  13.5 us (94%)
  between operations  0.64 us (4%)
    pallas_call x1, Pallas kernels, shards(): pl.pallas_call(functools.partial(kernel, rows, levels), out_shape=[pltpu....  12.7 us
    pallas_call x1, Pallas kernels, shards(): pl.pallas_call(write_out, out_shape=[jax.ShapeDtypeStruct((levels * rows,...  0.82 us

profile of v2, /device:TPU:24, one launch (start us, length us, event | category | flops | bytes accessed | tf_op | source)
XLA Modules:
  0.0 14.2 jit_solution(1500422733791244020)
XLA Ops:
  0.6 12.7 %shard_map.84 = (f32[256,128]{1,0:T(8,128)S(1)}, f32[256,128]{1,0:T(8,128)S(1)}, f32[256,128]{1,0:T(8,128)S(1)}, f32[256,128]{1,0:T(8,128)S(1)}) custom-call(f32[256,128]{1,0:T(8,128)} %bitcast.9, f32[256,128]{1,0:T(8,128)} %bitcast.10, f32[256,128]{1,0:T(8,128)} %bitcast.11, f32[256,128]{1,0:T(8,128)} %bitcast.12, s32[256,128]{1,0:T(8,128)} %bitcast.13), custom_call_target="tpu_custom_call" | custom-call | tf_op jit(solution)/shard_map/pallas_call | solution.py:397
  13.4 0.8 %shard_map.85 = (f32[256,128]{1,0:T(8,128)}, f32[256,128]{1,0:T(8,128)}, f32[256,128]{1,0:T(8,128)}, f32[256,128]{1,0:T(8,128)}) custom-call(f32[256,128]{1,0:T(8,128)S(1)} %get-tuple-element.12.refs_0_, f32[256,128]{1,0:T(8,128)S(1)} %get-tuple-element.13.refs_1_, f32[256,128]{1,0:T(8,128)S(1)} %get-tuple-element.14.refs_2_, ...), custom_call_target="tpu_custom_call" | custom-call | tf_op jit(solution)/shard_map/pallas_call | solution.py:426

commit v3 on v2

--- a/solution.py
+++ b/solution.py
@@ -37,14 +37,14 @@
 
 
 def blocks(first, count, size, body):
-    number = (count + size - 1) // size
-
-    for b in range(number):
-        body(min(first + b * size, first + count - size))
+    start = first
+    while start < first + count:
+        body(start, min(size, first + count - start))
+        start += size
 
 
 def pressure_pass(temp, salt, load, first, count, size):
-    def body(start):
+    def body(start, size):
         rows = pl.ds(start, size)
         total = (0.8 * LAYER_DEPTH) * salt[rows] - (0.2 * LAYER_DEPTH) * temp[rows]
         level = lax.broadcasted_iota(jnp.int32, total.shape, 1)
@@ -58,7 +58,7 @@
 
 
 def velocity_pass(load, wet, east, north, east_to, north_to, first, count, size):
-    def body(start):
+    def body(start, size):
         rows = pl.ds(start, size)
         here = load[rows]
         width = here.shape[2]
@@ -72,7 +72,7 @@
 
 
 def tracer_pass(tracers, wet, east, north, tracers_to, first, count, size):
-    def body(start):
+    def body(start, size):
         rows = pl.ds(start, size)
         around = pl.ds(start - 1, size + 2)
         sea = wet[around]
@@ -98,17 +98,26 @@
     blocks(first, count, size, body)
 
 
-def run_steps(ext, work, rows, size):
+def run_steps(ext, work, rows, size, parts):
     every = rows + 2 * HALO
-    load = work.at[0]
     wet = ext.at[4]
     held = [ext.at[f] for f in range(4)]
     for step in range(STEPS):
+        load = work.at[9 * step]
         to = [work.at[1 + 4 * step + f] for f in range(4)]
-        edge = 2 * step
-        pressure_pass(held[0], held[1], load, edge, every - 2 * edge, size)
-        velocity_pass(load, wet, held[2], held[3], to[2], to[3], edge + 1, every - 2 * edge - 2, size)
-        tracer_pass(held[:2], wet, to[2], to[3], to[:2], edge + 2, every - 2 * edge - 4, size)
+        for reach in range(3):
+            edge = 2 * step + reach
+            whole = (edge, every - 2 * edge)
+            inner = (edge + HALO, every - 2 * edge - 2 * HALO)
+            outer = [(edge, HALO), (every - edge - HALO, HALO)]
+            todo = {"inner": [inner], "outer": outer, "whole": [whole]}[parts]
+            for first, count in todo:
+                if reach == 0:
+                    pressure_pass(held[0], held[1], load, first, count, size)
+                elif reach == 1:
+                    velocity_pass(load, wet, held[2], held[3], to[2], to[3], first, count, size)
+                else:
+                    tracer_pass(held[:2], wet, to[2], to[3], to[:2], first, count, size)
         held = to
 
 
@@ -178,31 +187,6 @@
                 value = staged_wet[pl.ds(r, levels, stride=rows), :].astype(jnp.float32)
             ext[f, HALO + r] = value
 
-    pl.semaphore_wait(barrier, 3 + jnp.minimum(lat, 1))
-
-    north_base = HALO + rows
-    row_north = pltpu.make_async_remote_copy(
-        src_ref=ext.at[:, pl.ds(rows, HALO)],
-        dst_ref=ext.at[:, pl.ds(top * north_base, HALO)],
-        send_sem=row_send.at[0],
-        recv_sem=row_recv.at[top],
-        device_id=north_id,
-        device_id_type=MESH,
-    )
-    row_south = pltpu.make_async_remote_copy(
-        src_ref=ext.at[:, pl.ds(HALO, HALO)],
-        dst_ref=ext.at[:, pl.ds(north_base, HALO)],
-        send_sem=row_send.at[1],
-        recv_sem=row_recv.at[1],
-        device_id=south_id,
-        device_id_type=MESH,
-    )
-    row_north.start()
-
-    @pl.when(has_south)
-    def _():
-        row_south.start()
-
     width = ext.shape[-1]
     slot_lanes = 2 * HALO
     groups = rows // HALO
@@ -225,6 +209,25 @@
     packed[0] = halves[0]
     packed[1 + groups] = halves[1]
 
+    pl.semaphore_wait(barrier, 3 + jnp.minimum(lat, 1))
+
+    north_base = HALO + rows
+    row_north = pltpu.make_async_remote_copy(
+        src_ref=ext.at[:, pl.ds(rows, HALO)],
+        dst_ref=ext.at[:, pl.ds(top * north_base, HALO)],
+        send_sem=row_send.at[0],
+        recv_sem=row_recv.at[top],
+        device_id=north_id,
+        device_id_type=MESH,
+    )
+    row_south = pltpu.make_async_remote_copy(
+        src_ref=ext.at[:, pl.ds(HALO, HALO)],
+        dst_ref=ext.at[:, pl.ds(north_base, HALO)],
+        send_sem=row_send.at[1],
+        recv_sem=row_recv.at[1],
+        device_id=south_id,
+        device_id_type=MESH,
+    )
     to_left = pltpu.make_async_remote_copy(
         src_ref=packed,
         dst_ref=from_right,
@@ -241,13 +244,21 @@
         device_id=right_id,
         device_id_type=MESH,
     )
+
     to_left.start()
     to_right.start()
+    row_north.start()
+
+    @pl.when(has_south)
+    def _():
+        row_south.start()
 
     @pl.when(lat == 0)
     def _():
         ext[:, 0:HALO] = jnp.zeros((FIELDS, HALO, levels, width), jnp.float32)
         corner[0] = jnp.zeros((2, levels, width), jnp.float32)
+
+    run_steps(ext, main_work, rows, 8, "inner")
 
     to_left.wait_recv()
     to_right.wait_recv()
@@ -278,30 +289,6 @@
     @pl.when(has_south)
     def _():
         corner_south.start()
-
-    row_south.wait_recv()
-
-    @pl.when(has_south)
-    def _():
-        pltpu.make_async_remote_copy(
-            src_ref=ext.at[:, pl.ds(rows, HALO)],
-            dst_ref=ext.at[:, pl.ds(0, HALO)],
-            send_sem=row_send.at[0],
-            recv_sem=row_recv.at[0],
-            device_id=north_id,
-            device_id_type=MESH,
-        ).wait_recv()
-
-    @pl.when(at_top)
-    def _():
-        for f in range(FIELDS):
-            turned = swap_lanes(ext[f, north_base : north_base + HALO], width - 1)
-            if f in (2, 3):
-                turned = -turned
-            for i in range(HALO):
-                ext[f, north_base + i] = turned[HALO - 1 - i]
-
-    run_steps(ext, main_work, rows, 8)
 
     def stitch(own, piece, slot):
         spot = lane_iota(own.shape)
@@ -322,6 +309,46 @@
             r = HALO + slots * half + slot
             seam[4, r] = stitch(ext[4, r], piece, slot)
 
+    run_steps(seam, seam_work, rows, 8, "inner")
+
+    outs = (temp_out, salt_out, east_out, north_out)
+
+    def finish(some):
+        for f, out in enumerate(outs):
+            for r in some:
+                edge = seam_work[5 + f, HALO + r]
+                spot = lane_iota(edge.shape)
+                value = main_work[5 + f, HALO + r]
+                value = jnp.where(spot < HALO, edge, value)
+                value = jnp.where(spot >= width - HALO, pltpu.roll(edge, slot_lanes, 1), value)
+                out[pl.ds(r, levels, stride=rows), :] = value
+
+    finish(range(HALO, rows - HALO))
+
+    row_south.wait_recv()
+
+    @pl.when(has_south)
+    def _():
+        pltpu.make_async_remote_copy(
+            src_ref=ext.at[:, pl.ds(rows, HALO)],
+            dst_ref=ext.at[:, pl.ds(0, HALO)],
+            send_sem=row_send.at[0],
+            recv_sem=row_recv.at[0],
+            device_id=north_id,
+            device_id_type=MESH,
+        ).wait_recv()
+
+    @pl.when(at_top)
+    def _():
+        for f in range(FIELDS):
+            turned = swap_lanes(ext[f, north_base : north_base + HALO], width - 1)
+            if f in (2, 3):
+                turned = -turned
+            for i in range(HALO):
+                ext[f, north_base + i] = turned[HALO - 1 - i]
+
+    run_steps(ext, main_work, rows, 8, "outer")
+
     corner_south.wait_recv()
 
     @pl.when(has_south)
@@ -352,16 +379,8 @@
             slot = i if side else slots - HALO + i
             seam[4, base + i] = stitch(ext[4, base + i], sea, slot)
 
-    run_steps(seam, seam_work, rows, 8)
-
-    for f, out in enumerate((temp_out, salt_out, east_out, north_out)):
-        for r in range(rows):
-            edge = seam_work[5 + f, HALO + r]
-            spot = lane_iota(edge.shape)
-            value = main_work[5 + f, HALO + r]
-            value = jnp.where(spot < HALO, edge, value)
-            value = jnp.where(spot >= width - HALO, pltpu.roll(edge, slot_lanes, 1), value)
-            out[pl.ds(r, levels, stride=rows), :] = value
+    run_steps(seam, seam_work, rows, 8, "outer")
+    finish([*range(HALO), *range(rows - HALO, rows)])
 
     row_north.wait_send()
     to_left.wait_send()
@@ -404,8 +423,8 @@
             pltpu.VMEM((levels * rows, columns), jnp.int32),
             vmem(FIELDS, every),
             vmem(FIELDS, every),
-            vmem(9, every),
-            vmem(9, every),
+            vmem(10, every),
+            vmem(10, every),
             vmem(pieces),
             vmem(pieces),
             vmem(pieces),

time: 14.3 us -> 12.2 us (0.85)
  the two profiles are of different devices: /device:TPU:24 before, /device:TPU:0 now
where the time goes in v3:
time: 12.2 us; the launch traced here: 12 us
  Pallas kernels  11.4 us (93%)
  between operations  0.64 us (5%)
    pallas_call x1, Pallas kernels, shards(): pl.pallas_call(functools.partial(kernel, rows, levels), out_shape=[pltpu....  10.5 us
    pallas_call x1, Pallas kernels, shards(): pl.pallas_call(write_out, out_shape=[jax.ShapeDtypeStruct((levels * rows,...  0.82 us

profile of v3, /device:TPU:0, one launch (start us, length us, event | category | flops | bytes accessed | tf_op | source)
XLA Modules:
  0.0 12.0 jit_solution(9921666231759513979)
XLA Ops:
  0.6 10.5 %shard_map.84 = (f32[256,128]{1,0:T(8,128)S(1)}, f32[256,128]{1,0:T(8,128)S(1)}, f32[256,128]{1,0:T(8,128)S(1)}, f32[256,128]{1,0:T(8,128)S(1)}) custom-call(f32[256,128]{1,0:T(8,128)} %bitcast.9, f32[256,128]{1,0:T(8,128)} %bitcast.10, f32[256,128]{1,0:T(8,128)} %bitcast.11, f32[256,128]{1,0:T(8,128)} %bitcast.12, s32[256,128]{1,0:T(8,128)} %bitcast.13), custom_call_target="tpu_custom_call" | custom-call | tf_op jit(solution)/shard_map/pallas_call | solution.py:416
  11.2 0.8 %shard_map.85 = (f32[256,128]{1,0:T(8,128)}, f32[256,128]{1,0:T(8,128)}, f32[256,128]{1,0:T(8,128)}, f32[256,128]{1,0:T(8,128)}) custom-call(f32[256,128]{1,0:T(8,128)S(1)} %get-tuple-element.12.refs_0_, f32[256,128]{1,0:T(8,128)S(1)} %get-tuple-element.13.refs_1_, f32[256,128]{1,0:T(8,128)S(1)} %get-tuple-element.14.refs_2_, ...), custom_call_target="tpu_custom_call" | custom-call | tf_op jit(solution)/shard_map/pallas_call | solution.py:445

commit v4 on v3

--- a/solution.py
+++ b/solution.py
@@ -258,7 +258,7 @@
         ext[:, 0:HALO] = jnp.zeros((FIELDS, HALO, levels, width), jnp.float32)
         corner[0] = jnp.zeros((2, levels, width), jnp.float32)
 
-    run_steps(ext, main_work, rows, 8, "inner")
+    run_steps(ext, main_work, rows, 16, "inner")
 
     to_left.wait_recv()
     to_right.wait_recv()
@@ -309,7 +309,7 @@
             r = HALO + slots * half + slot
             seam[4, r] = stitch(ext[4, r], piece, slot)
 
-    run_steps(seam, seam_work, rows, 8, "inner")
+    run_steps(seam, seam_work, rows, 16, "inner")
 
     outs = (temp_out, salt_out, east_out, north_out)
 
@@ -347,7 +347,7 @@
             for i in range(HALO):
                 ext[f, north_base + i] = turned[HALO - 1 - i]
 
-    run_steps(ext, main_work, rows, 8, "outer")
+    run_steps(ext, main_work, rows, 16, "outer")
 
     corner_south.wait_recv()
 
@@ -379,7 +379,7 @@
             slot = i if side else slots - HALO + i
             seam[4, base + i] = stitch(ext[4, base + i], sea, slot)
 
-    run_steps(seam, seam_work, rows, 8, "outer")
+    run_steps(seam, seam_work, rows, 16, "outer")
     finish([*range(HALO), *range(rows - HALO, rows)])
 
     row_north.wait_send()

time: 12.2 us -> 12.2 us (level)
  no operation moved by 1% of the time
where the time goes in v4:
time: 12.2 us; the launch traced here: 12 us
  Pallas kernels  11.4 us (93%)
  between operations  0.64 us (5%)
    pallas_call x1, Pallas kernels, shards(): pl.pallas_call(functools.partial(kernel, rows, levels), out_shape=[pltpu....  10.5 us
    pallas_call x1, Pallas kernels, shards(): pl.pallas_call(write_out, out_shape=[jax.ShapeDtypeStruct((levels * rows,...  0.82 us

profile of v4, /device:TPU:0, one launch (start us, length us, event | category | flops | bytes accessed | tf_op | source)
XLA Modules:
  0.0 12.0 jit_solution(8330123725202850098)
XLA Ops:
  0.6 10.5 %shard_map.84 = (f32[256,128]{1,0:T(8,128)S(1)}, f32[256,128]{1,0:T(8,128)S(1)}, f32[256,128]{1,0:T(8,128)S(1)}, f32[256,128]{1,0:T(8,128)S(1)}) custom-call(f32[256,128]{1,0:T(8,128)} %bitcast.9, f32[256,128]{1,0:T(8,128)} %bitcast.10, f32[256,128]{1,0:T(8,128)} %bitcast.11, f32[256,128]{1,0:T(8,128)} %bitcast.12, s32[256,128]{1,0:T(8,128)} %bitcast.13), custom_call_target="tpu_custom_call" | custom-call | tf_op jit(solution)/shard_map/pallas_call | solution.py:416
  11.2 0.8 %shard_map.85 = (f32[256,128]{1,0:T(8,128)}, f32[256,128]{1,0:T(8,128)}, f32[256,128]{1,0:T(8,128)}, f32[256,128]{1,0:T(8,128)}) custom-call(f32[256,128]{1,0:T(8,128)S(1)} %get-tuple-element.12.refs_0_, f32[256,128]{1,0:T(8,128)S(1)} %get-tuple-element.13.refs_1_, f32[256,128]{1,0:T(8,128)S(1)} %get-tuple-element.14.refs_2_, ...), custom_call_target="tpu_custom_call" | custom-call | tf_op jit(solution)/shard_map/pallas_call | solution.py:445
